TPU v7x, 256 devices: a whole 4x4x8 slice. The times are simulated.
256 devices in a mesh: dp: 64 (over z, y, core), shard: 4 (over x).
Axes of the slice: x: 4, y: 4, z: 8, core: 2. Of those that a mesh axis runs over, the one named last changes fastest.
Arguments:
- gradients: float32 [1024, 256, 256], P('dp', 'shard'), may hold values from -6 to 6
- left_stats: float32 [1024, 256, 256], P('dp', 'shard'), may hold values from -3 to 100, as said below
- right_stats: float32 [1024, 256, 256], P('dp', 'shard'), may hold values from -3 to 100, as said below
- left_roots: float32 [1024, 256, 256], P('dp', 'shard'), may hold values from -0.1 to 3, as said below
- right_roots: float32 [1024, 256, 256], P('dp', 'shard'), may hold values from -0.1 to 3, as said below
- due_factors: int32 [1024], replicated, may hold values from 0 to 2047, as said below
- block_owner: int32 [1024], replicated, may hold values from 0 to 1023, as said below
Outputs:
- new_left: float32 [1024, 256, 256], P('dp', 'shard')
- new_right: float32 [1024, 256, 256], P('dp', 'shard')
- new_left_roots: float32 [1024, 256, 256], P('dp', 'shard')
- new_right_roots: float32 [1024, 256, 256], P('dp', 'shard')
- update: float32 [1024, 256, 256], P('dp', 'shard')
Inputs may be any that keep to these rules, and one draw needn't show every extreme that they name: `block_owner`: each of the 1024 storage slots appears once; slot s is kept by index s // 16 of dp. `due_factors`: distinct values 2 b + side for block b, side 0 naming the left factor and 1 the right; the due factors of the blocks kept by one index of dp number at most 32, and exactly that many on some index. `left_stats`: each block is symmetric positive definite. `right_stats`: each block is symmetric positive definite. `left_roots`: each block is symmetric positive definite. `right_roots`: each block is symmetric positive definite.
All inputs are finite; a program needn't handle non-finite values.
Results may differ from a plain program's by a relative error of at most 0.00017.
Values sent between devices are 32-bit elements; how exact they have to be, the bound alone decides.
A program may use at most 64 MiB of HBM per device.

v0:
```python
import jax
import jax.numpy as jnp
from jax import lax
from jax.sharding import PartitionSpec as P

ITERS = 10


STAT_DECAY = 0.95
PRECISE = lax.Precision.HIGHEST


def newton_root(matrices):
    extent = matrices.shape[-1]
    identity = jnp.eye(extent, dtype=jnp.float32)
    frobenius = jnp.sqrt(jnp.sum(matrices * matrices, axis=(-2, -1)))
    matrix = matrices / frobenius[..., None, None]
    iterate = identity * (frobenius ** (-0.25))[..., None, None]

    def newton_step(counter, carry):
        iterate, matrix = carry
        factor = (5.0 * identity - matrix) * 0.25
        iterate = jnp.einsum("...ij,...jk->...ik", iterate, factor, precision=PRECISE)
        square = jnp.einsum("...ij,...jk->...ik", factor, factor, precision=PRECISE)
        fourth = jnp.einsum("...ij,...jk->...ik", square, square, precision=PRECISE)
        matrix = jnp.einsum("...ij,...jk->...ik", fourth, matrix, precision=PRECISE)
        return (iterate, matrix)

    iterate, matrix = lax.fori_loop(0, ITERS, newton_step, (iterate, matrix))
    return iterate


def plan(due_factors, block_owner, groups, per_group):
    block_count = block_owner.shape[0]
    blocks = due_factors // 2
    side_of = due_factors % 2
    matches = blocks[:, None] == jnp.arange(block_count, dtype=jnp.int32)[None, :]
    slot_of = jnp.sum(jnp.where(matches, block_owner[None, :], 0), axis=1)
    storage = 2 * slot_of + side_of
    positions = jnp.sum((storage[None, :] < storage[:, None]).astype(jnp.int32), axis=1)
    owners = storage // per_group
    starts = jnp.sum((owners[None, :] < owners[:, None]).astype(jnp.int32), axis=1)
    local_ids = storage % per_group
    targets = positions % groups
    places = (positions - starts) // groups
    return (positions, owners, local_ids, targets, places)


def local(gradients, left_stats, right_stats, left_roots, right_roots, due_factors, block_owner):
    blocks_here, quarter, extent = gradients.shape
    members = lax.axis_size("shard")
    groups = lax.axis_size("dp")
    gathered = lax.all_gather(gradients, "shard", axis=1, tiled=True)
    shard_index = lax.axis_index("shard")
    columns = lax.dynamic_slice_in_dim(gathered, shard_index * quarter, quarter, 2)
    left_gram = jnp.einsum("bik,bjk->bij", gradients, gathered, precision=PRECISE)
    right_gram = jnp.einsum("bki,bkj->bij", columns, gathered, precision=PRECISE)
    new_left = STAT_DECAY * left_stats + (1.0 - STAT_DECAY) * left_gram
    new_right = STAT_DECAY * right_stats + (1.0 - STAT_DECAY) * right_gram
    per_group = 2 * blocks_here
    positions, owners, local_ids, targets, places = plan(
        due_factors, block_owner, groups, per_group
    )
    myself = lax.axis_index("dp")
    is_mine = owners == myself
    factor_ids = jnp.arange(per_group, dtype=jnp.int32)
    own_match = is_mine[None, :] & (local_ids[None, :] == factor_ids[:, None])
    is_due = jnp.any(own_match, axis=1)
    statistics = jnp.stack([new_left, new_right], axis=1).reshape(per_group, quarter, extent)
    due_each = due_factors.shape[0] // (groups * members)
    capacity = (per_group + groups - 1) // groups
    slot_count = groups * capacity
    slot_ids = jnp.arange(slot_count, dtype=jnp.int32)
    addresses = targets * capacity + places
    sending = is_mine[None, :] & (addresses[None, :] == slot_ids[:, None])
    occupied = jnp.any(sending, axis=1)
    picked = jnp.sum(jnp.where(sending, local_ids[None, :], 0), axis=1)
    outgoing = jnp.where(occupied[:, None, None], jnp.take(statistics, picked, axis=0), 0.0)
    incoming = lax.all_to_all(outgoing, "dp", split_axis=0, concat_axis=0, tiled=True)
    wanted = myself + groups * jnp.arange(members * due_each, dtype=jnp.int32)
    chosen_due = positions[None, :] == wanted[:, None]
    sources = jnp.sum(jnp.where(chosen_due, (owners * capacity + places)[None, :], 0), axis=1)
    gathered_rows = jnp.take(incoming, sources, axis=0).reshape(members, due_each, quarter, extent)
    root_stack = newton_root(
        lax.all_to_all(gathered_rows, "shard", split_axis=0, concat_axis=2, tiled=True)
    )
    results = lax.all_to_all(root_stack, "shard", split_axis=2, concat_axis=0, tiled=True)
    results = results.reshape(members * due_each, quarter, extent)
    returning = jnp.zeros_like(incoming).at[sources].set(results)
    returned = lax.all_to_all(returning, "dp", split_axis=0, concat_axis=0, tiled=True)
    address_of = jnp.sum(jnp.where(own_match, addresses[None, :], 0), axis=1)
    refreshed = jnp.take(returned, address_of, axis=0)
    old_roots = jnp.stack([left_roots, right_roots], axis=1).reshape(per_group, quarter, extent)
    root_pairs = jnp.where(is_due[:, None, None], refreshed, old_roots).reshape(
        blocks_here, 2, quarter, extent
    )
    new_left_roots = root_pairs[:, 0]
    new_right_roots = root_pairs[:, 1]
    middle = jnp.einsum("bik,bkj->bij", new_left_roots, gathered, precision=PRECISE)
    update = jnp.einsum(
        "bik,bkj->bij",
        middle,
        lax.all_gather(new_right_roots, "shard", axis=1, tiled=True),
        precision=PRECISE,
    )
    return (new_left, new_right, new_left_roots, new_right_roots, update)


def solution(mesh):
    in_specs = (
        P("dp", "shard", None),
        P("dp", "shard", None),
        P("dp", "shard", None),
        P("dp", "shard", None),
        P("dp", "shard", None),
        P(),
        P(),
    )
    out_specs = (
        P("dp", "shard", None),
        P("dp", "shard", None),
        P("dp", "shard", None),
        P("dp", "shard", None),
        P("dp", "shard", None),
    )
    return jax.shard_map(local, mesh=mesh, in_specs=in_specs, out_specs=out_specs, check_vma=False)
```

profile of v0, /device:TPU:104, one launch (start us, length us, event | category | flops | bytes accessed | tf_op | source)
XLA Modules:
  0.0 459.5 jit_solution(5054292471346092733)
XLA Ops:
  12.3 50.1 %all-gather.4.cloned.1.call-done = f32[16,256,256]{2,1,0:T(8,128)} async-done(((f32[16,64,256]{2,1,0:T(8,128)}), f32[16,256,256]{2,1,0:T(8,128)}) %all-gather.4.cloned.1.call-update) | async-done | bytes 4194320 | tf_op jit(solution)/shard_map/all_gather | solution.py:53
  62.4 7.1 %fusion.21 = f32[16,64,256]{2,1,0:T(8,128)S(1)} fusion(f32[16,64,256]{2,1,0:T(8,128)} %param.9, f32[16,256,256]{2,1,0:T(8,128)} %all-gather.4.cloned.1.call-done, f32[16,64,256]{2,1,0:T(8,128)} %param.10), kind=kOutput, calls=%fused_computation.35 | convolution fusion | flops 806092800 | bytes 7340032 | tf_op jit(solution)/shard_map/bik,bjk->bij/dot_general | solution.py:56
  69.5 4.3 fusion.22
  74.8 2.8 gather_fusion
  77.6 4.7 %select_select_fusion = f32[64,64,256]{2,1,0:T(8,128)} fusion(f32[64,64,256]{2,1,0:T(8,128)} %gather_fusion, pred[64]{0:T(512)(128)(4,1)S(1)} %compare_and_fusion.1, pred[64]{0:T(512)(128)(4,1)S(1)} %fusion.27), kind=kLoop, calls=%fused_computation.23 | loop fusion | flops 2097152 | bytes 8388736 | tf_op jit(solution)/shard_map/jit(_where)/select_n | solution.py:78
  82.2 10.5 %all-to-all-start = ((f32[64,64,256]{2,1,0:T(8,128)}), f32[64,64,256]{2,1,0:T(8,128)}, u32[]{:S(2)}, u32[]{:S(2)}) async-start(f32[64,64,256]{2,1,0:T(8,128)} %select_select_fusion), calls=%async_computation | async-start | bytes 8388608 | tf_op jit(solution)/shard_map/all_to_all | solution.py:79
  93.1 93.0 %all-to-all-done = f32[64,64,256]{2,1,0:T(8,128)} async-done(((f32[64,64,256]{2,1,0:T(8,128)}), f32[64,64,256]{2,1,0:T(8,128)}, u32[]{:S(2)}, u32[]{:S(2)}) %all-to-all-start) | async-done | bytes 4194336 | tf_op jit(solution)/shard_map/all_to_all | solution.py:79
  186.1 2.8 gather_fusion.1
  190.1 3.7 all-to-all-start.1
  193.8 15.3 %all-to-all-done.1 = f32[4,4,64,256]{3,2,1,0:T(8,128)S(1)} async-done(((f32[4,4,64,256]{3,2,1,0:T(8,128)}), f32[4,4,64,256]{3,2,1,0:T(8,128)S(1)}, u32[]{:S(2)}, u32[]{:S(2)}) %all-to-all-start.1) | async-done | bytes 1048608 | tf_op jit(solution)/shard_map/all_to_all | solution.py:85
  209.7 56.9 %while.13 = (s32[]{:T(128)}, f32[1,4,256,256]{2,3,1,0:T(8,128)S(1)}, f32[1,4,256,256]{3,2,1,0:T(8,128)S(1)}, s32[]{:T(128)}) while((s32[]{:T(128)}, f32[1,4,256,256]{2,3,1,0:T(8,128)S(1)}, f32[1,4,256,256]{3,2,1,0:T(8,128)S(1)}, s32[]{:T(128)}) %tuple.32), condition=%wide.region_10.11_spmd.clone, body=%wide.region_9.10_spmd.clone.sunk | while | flops 3222405120 | bytes 15466549 | solution.py:29
  212.4 1.9 convolution_bitcast_fusion.4
  218.1 1.9 convolution_bitcast_fusion.4
  223.8 1.9 convolution_bitcast_fusion.4
  229.5 1.9 convolution_bitcast_fusion.4
  267.1 17.1 %all_to_all.43 = f32[1,4,256,256]{3,1,0,2:T(4,128)S(1)} all-to-all(f32[1,4,256,256]{3,1,0,2:T(4,128)S(1)} %copy.55), channel_id=1, replica_groups=mesh['dp'=64,'shard'=4] {'shard'}, dimensions={2} | all-to-all | bytes 2097152 | tf_op jit(solution)/shard_map/all_to_all | solution.py:87
  284.5 2.5 broadcast_in_dim.133
  287.0 3.0 scatter_fusion
  290.0 9.0 %all-to-all-start.3 = ((f32[64,64,256]{2,1,0:T(8,128)}), f32[64,64,256]{2,1,0:T(8,128)}, u32[]{:S(2)}, u32[]{:S(2)}) async-start(f32[64,64,256]{2,1,0:T(8,128)} %scatter_fusion), calls=%async_computation.3 | async-start | bytes 8388608 | tf_op jit(solution)/shard_map/all_to_all | solution.py:90
  300.0 92.4 %all-to-all-done.3 = f32[64,64,256]{2,1,0:T(8,128)} async-done(((f32[64,64,256]{2,1,0:T(8,128)}), f32[64,64,256]{2,1,0:T(8,128)}, u32[]{:S(2)}, u32[]{:S(2)}) %all-to-all-start.3) | async-done | bytes 4194336 | tf_op jit(solution)/shard_map/all_to_all | solution.py:90
  392.4 2.9 gather_fusion.2
  398.5 5.2 %fusion.48 = f32[16,64,256]{2,1,0:T(8,128)S(1)} fusion(f32[16,64,256]{2,1,0:T(8,128)S(1)} %get-tuple-element.47, f32[16,256,256]{2,1,0:T(8,128)} %all-gather.4.cloned.1.call-done), kind=kOutput, calls=%fused_computation.106 | convolution fusion | flops 805306368 | bytes 6291456 | tf_op jit(solution)/shard_map/bik,bkj->bij/dot_general | solution.py:99
  403.8 43.0 %all-gather.6.cloned.1.call-done = f32[16,1,256,256]{3,2,0,1:T(8,128)} async-done(((f32[16,1,64,256]{3,2,0,1:T(8,128)}), f32[16,1,256,256]{3,2,0,1:T(8,128)}) %all-gather.6.cloned.1.call-update) | async-done | bytes 4194320 | tf_op jit(solution)/shard_map/all_gather | solution.py:103
  446.8 5.8 %fusion.14 = f32[16,64,256]{2,1,0:T(8,128)} fusion(f32[16,64,256]{2,1,0:T(8,128)S(1)} %fusion.48, f32[16,1,256,256]{3,2,0,1:T(8,128)} %all-gather.6.cloned.1.call-done), kind=kOutput, calls=%fused_computation.21 | convolution fusion | flops 805306368 | bytes 6291456 | tf_op jit(solution)/shard_map/bik,bkj->bij/dot_general | solution.py:100
  (122 shorter events, 61.7 us)
Async XLA Ops:
  7.2 62.3 %copy-start.4 = (f32[16,64,256]{2,1,0:T(8,128)S(1)}, f32[16,64,256]{2,1,0:T(8,128)}, u32[]{:S(2)}) copy-start(f32[16,64,256]{2,1,0:T(8,128)} %param.11) | copy-start | bytes 3145732
  7.2 55.3 %all-gather.4.cloned.1.call-start = ((), (), s32[]{:S(2)}) async-start(), calls=%async_computation.4 | async-start | bytes 5242880 | tf_op jit(solution)/shard_map/all_gather | solution.py:53
  62.4 7.1 %copy-start = (f32[16,256,256]{2,1,0:T(8,128)S(1)}, f32[16,256,256]{2,1,0:T(8,128)}, u32[]{:S(2)}) copy-start(f32[16,256,256]{2,1,0:T(8,128)} %all-gather.4.cloned.1.call-done) | copy-start | bytes 12582916
  69.5 4.5 copy-start.1
  73.8 1.0 copy-start.2
  82.2 103.9 %all-to-all-start = ((f32[64,64,256]{2,1,0:T(8,128)}), f32[64,64,256]{2,1,0:T(8,128)}, u32[]{:S(2)}, u32[]{:S(2)}) async-start(f32[64,64,256]{2,1,0:T(8,128)} %select_select_fusion), calls=%async_computation | async-start | bytes 8388608 | tf_op jit(solution)/shard_map/all_to_all | solution.py:79
  190.1 19.0 %all-to-all-start.1 = ((f32[4,4,64,256]{3,2,1,0:T(8,128)}), f32[4,4,64,256]{3,2,1,0:T(8,128)S(1)}, u32[]{:S(2)}, u32[]{:S(2)}) async-start(f32[4,4,64,256]{3,2,1,0:T(8,128)} %broadcast_select_fusion), calls=%async_computation.1 | async-start | bytes 2097152 | tf_op jit(solution)/shard_map/all_to_all | solution.py:85
  290.0 102.4 %all-to-all-start.3 = ((f32[64,64,256]{2,1,0:T(8,128)}), f32[64,64,256]{2,1,0:T(8,128)}, u32[]{:S(2)}, u32[]{:S(2)}) async-start(f32[64,64,256]{2,1,0:T(8,128)} %scatter_fusion), calls=%async_computation.3 | async-start | bytes 8388608 | tf_op jit(solution)/shard_map/all_to_all | solution.py:90
  299.0 96.2 %copy-start.5 = (f32[16,64,256]{2,1,0:T(8,128)S(1)}, f32[16,64,256]{2,1,0:T(8,128)}, u32[]{:S(2)}) copy-start(f32[16,64,256]{2,1,0:T(8,128)} %param.13) | copy-start | bytes 3145732
  299.0 147.8 %all-gather.6.cloned.1.call-start = ((), (), s32[]{:S(2)}) async-start(), calls=%async_computation.5 | async-start | bytes 5242880 | tf_op jit(solution)/shard_map/all_gather | solution.py:103
  398.5 54.1 %copy-start.3 = (f32[16,64,256]{2,1,0:T(8,128)}, f32[16,64,256]{2,1,0:T(8,128)S(1)}, u32[]{:S(2)}) copy-start(f32[16,64,256]{2,1,0:T(8,128)S(1)} %get-tuple-element.47) | copy-start | bytes 3145732
Sparse Core Ops, SparseCore 0:
  9.8 52.5 all-gather.3
  398.7 48.1 all-gather.5
where the time goes:
time: 462 us; the launch traced here: 460 us
  waiting for transfers between devices  295 us (64%)
  matrix products  77 us (17%)
  starting transfers between devices  23.6 us (5%)
  local copies, waits for them, and re-layouts  19.2 us (4%)
  blocking collectives  17.1 us (4%)
  between operations  14.3 us (3%)
  other arithmetic  13.1 us (3%)
    all_to_all x1, waiting for transfers between devices, local(): lax.all_to_all(outgoing, 'dp', split_axis=0, concat_axis=0, tiled=True)  93 us
    all_to_all x1, waiting for transfers between devices, local(): lax.all_to_all(returning, 'dp', split_axis=0, concat_axis=0, tiled=True)  92.4 us
    all_gather x1, waiting for transfers between devices, local(): gathered = lax.all_gather(gradients, 'shard', axis=1, tiled=True)  50.1 us
    all_gather x1, waiting for transfers between devices, local(): lax.all_gather(new_right_roots, 'shard', axis=1, tiled=True)  43 us
    dot_general x10, matrix products, newton_step(): jnp.einsum('...ij,...jk->...ik', iterate, factor, precision=PRECISE)  18.9 us
    all_to_all x1, blocking collectives, local(): lax.all_to_all(root_stack, 'shard', split_axis=2, concat_axis=0, tiled=True)  17.1 us
    all_to_all x1, waiting for transfers between devices, local(): lax.all_to_all(gathered_rows, 'shard', split_axis=0, concat_axis=2, tiled...  15.3 us
    dot_general x10, matrix products, newton_step(): square = jnp.einsum('...ij,...jk->...ik', factor, factor, precision=PRECISE)  12.8 us
  transfers between devices with their start and end apart: 5, of which 5 were waited for; matrix products, arithmetic and copies ran while one was open for 2% of the time, Pallas kernels for 0%

commit v1 on v0

v1 whole, which is shorter than its diff:
```python
import functools

import jax
import jax.numpy as jnp
from jax import lax
from jax.experimental import pallas as pl
from jax.experimental.pallas import tpu as pltpu
from jax.sharding import PartitionSpec as P

ITERS = 10
STAT_DECAY = 0.95
MESH = pl.DeviceIdType.MESH
VMEM_LIMIT = 63 * 1024 * 1024
F32 = jnp.float32
BF16 = jnp.bfloat16


def mm(a, b):
    return jnp.dot(a, b, precision=lax.Precision.HIGH, preferred_element_type=F32)


def kernel(
    n,
    g, ls, rs, lr, rr, due, own,
    stats_out, roots_out,
    duev, ownv, gf, st, rt, sel, spk, pk, p, gg, rg, out, mk,
    fg, fs, fgg, fo,
    spread, mat, root,
    load_sem, own_sem, done_sem,
    g_send, g_recv, s_send, s_recv, q_send, q_recv, o_send, o_recv,
):
    blocks, quarter, extent = g.shape
    each = blocks // n
    half = extent // 2
    me = lax.axis_index("shard")
    group = lax.axis_index("dp")
    right = lax.rem(me + 1, n)
    left = lax.rem(me + n - 1, n)
    opposite = lax.rem(me + 2, n)
    sides = ((right, left), (left, right))

    def rows(index):
        return pl.ds(pl.multiple_of(index * quarter, quarter), quarter)

    def cols(d):
        return pl.ds(d * half, half)

    def remote(src, dst, send, recv, device):
        return pltpu.make_async_remote_copy(
            src_ref=src, dst_ref=dst, send_sem=send, recv_sem=recv,
            device_id=(group, device), device_id_type=MESH,
        )

    def g_copy(d, stage, j):
        device, origin = sides[d]
        return remote(*(
            (g.at[opposite * each + j, :, cols(d)], fg.at[d, j], g_send.at[d, 0, j], g_recv.at[d, 0, j], device),
            (g.at[device * each + j], gf.at[j, rows(me), :], g_send.at[d, 1, j], g_recv.at[d, 1, j], device),
            (fg.at[d, j], gf.at[j, rows(origin), cols(d)], g_send.at[d, 2, j], g_recv.at[d, 2, j], device),
        )[stage])

    def s_copy(d, stage, j):
        device, origin = sides[d]
        return remote(*(
            (spk.at[opposite * each + j, d], fs.at[d, j], s_send.at[d, 0, j], s_recv.at[d, 0, j], device),
            (spk.at[device * each + j], pk.at[me, j], s_send.at[d, 1, j], s_recv.at[d, 1, j], device),
            (fs.at[d, j], pk.at[origin, j, d], s_send.at[d, 2, j], s_recv.at[d, 2, j], device),
        )[stage])

    def q_copy(d, stage, j):
        device, origin = sides[d]
        return remote(*(
            (gg.at[:, j, rows(opposite), cols(d)], fgg.at[d, j], q_send.at[d, 0, j], q_recv.at[d, 0, j], device),
            (gg.at[:, j, rows(device), :], rg.at[:, me * each + j], q_send.at[d, 1, j], q_recv.at[d, 1, j], device),
            (fgg.at[d, j], rg.at[:, origin * each + j, :, cols(d)], q_send.at[d, 2, j], q_recv.at[d, 2, j], device),
        )[stage])

    def o_copy(d, stage, j):
        device, origin = sides[d]
        return remote(*(
            (out.at[:, j, rows(opposite), cols(d)], fo.at[d, j], o_send.at[d, 0, j], o_recv.at[d, 0, j], device),
            (out.at[:, j, rows(device), :], roots_out.at[:, me * each + j], o_send.at[d, 1, j], o_recv.at[d, 1, j], device),
            (fo.at[d, j], roots_out.at[:, origin * each + j, :, cols(d)], o_send.at[d, 2, j], o_recv.at[d, 2, j], device),
        )[stage])

    def begin(copy, j):
        for stage in (0, 1):
            for d in (0, 1):
                copy(d, stage, j).start()

    def forward(copy, j):
        for d in (0, 1):
            copy(d, 0, j).wait_recv()
            copy(d, 2, j).start()

    def arrived(copy, j):
        for d in (0, 1):
            for stage in (1, 2):
                copy(d, stage, j).wait_recv()

    def o_own(j):
        return pltpu.make_async_copy(
            out.at[:, j, rows(me), :], roots_out.at[:, me * each + j], done_sem.at[0, j]
        )

    def q_own(j):
        return pltpu.make_async_copy(
            gg.at[:, j, rows(me), :], rg.at[:, me * each + j], done_sem.at[1, j]
        )

    loads = [
        pltpu.make_async_copy(ref, place, load_sem.at[i])
        for i, (ref, place) in enumerate(
            ((due, duev), (own, ownv), (ls, st.at[0]), (rs, st.at[1]), (lr, rt.at[0]), (rr, rt.at[1]))
        )
    ]
    own_rows = pltpu.make_async_copy(
        g.at[pl.ds(me * each, each)], gf.at[:, rows(me), :], own_sem.at[0]
    )
    for load in loads:
        load.start()

    barrier = pltpu.get_barrier_semaphore()
    for device in (left, right):
        pl.semaphore_signal(barrier, inc=1, device_id=(group, device), device_id_type=MESH)
    pl.semaphore_wait(barrier, 2)

    begin(g_copy, 0)
    begin(g_copy, 1)
    own_rows.start()

    total = own.shape[1]
    for load in loads[:2]:
        load.wait()
    slots = group * blocks + lax.broadcasted_iota(jnp.int32, (blocks, total), 0)
    numbers = lax.broadcasted_iota(jnp.int32, (blocks, total), 1)
    stored = jnp.where(ownv[...] == slots, numbers, 0).astype(F32)
    number = jnp.sum(stored, axis=1, keepdims=True)
    entries = duev[...].astype(F32)
    for side in (0, 1):
        hit = jnp.where(entries == 2.0 * number + side, 1.0, 0.0)
        flag = jnp.max(hit, axis=1, keepdims=True)
        mk[side] = jnp.broadcast_to(flag, (blocks, half))

    for load in loads[2:]:
        load.wait()

    low_lanes = lax.broadcasted_iota(jnp.int32, (quarter, half), 1) < quarter

    @pl.loop(0, blocks)
    def _(b):
        second = lax.rem(jnp.where(b // each == right, me + 2, me + 1), n)
        for side in (0, 1):
            flag = mk[side, pl.ds(b, 1), :] > 0.5
            halves = []
            for d in (0, 1):
                value = jnp.where(
                    flag,
                    st[side, b, :, d * half:(d + 1) * half],
                    rt[side, b, :, d * half:(d + 1) * half],
                )
                sel[side, b, :, d * half:(d + 1) * half] = value
                halves.append(value)
            low = jnp.where(me // 2 == 0, halves[0], halves[1])
            low = jnp.where(lax.rem(me, 2) == 0, low, pltpu.roll(low, quarter, 1))
            high = jnp.where(second // 2 == 0, halves[0], halves[1])
            high = jnp.where(lax.rem(second, 2) == 1, high, pltpu.roll(high, quarter, 1))
            spk[b, side] = jnp.where(low_lanes, low, high)

    begin(s_copy, 0)
    begin(s_copy, 1)
    forward(g_copy, 0)
    forward(s_copy, 0)
    begin(g_copy, 2)
    begin(s_copy, 2)
    forward(g_copy, 1)
    forward(s_copy, 1)
    begin(g_copy, 3)
    begin(s_copy, 3)
    own_rows.wait()

    row_ids = lax.broadcasted_iota(jnp.int32, (extent, extent), 0)
    col_ids = lax.broadcasted_iota(jnp.int32, (extent, extent), 1)
    diagonal = row_ids == col_ids
    mat[...] = jnp.zeros_like(mat)
    root[...] = jnp.zeros_like(root)

    def partner(row):
        return lax.rem(row + jnp.where(row == left, 2, 1), n)

    def gram(j):
        arrived(g_copy, j)
        straight = gf[j]
        turned = straight.T
        gg[0, j] = mm(straight, turned)
        gg[1, j] = mm(turned, straight)
        begin(q_copy, j)
        q_own(j).start()

    def prepare(j, chain):
        arrived(s_copy, j)
        row_part, col_part = row_ids // quarter, col_ids // quarter
        other = lax.rem(row_part + jnp.where(row_part == left, 2, 1), n)
        known = (row_part == me) | (row_part == col_part) | (col_part == other)
        for i in (0, 1):
            for row in range(n):
                second = partner(row)
                packed = pk[row, j, i]
                turned_round = pltpu.roll(packed, quarter, 1)
                low = packed if row % 2 == 0 else turned_round
                high = jnp.where(lax.rem(second, 2) == 1, packed, turned_round)
                for d in (0, 1):
                    part = 2 * d + jnp.where(low_lanes, 0, 1)
                    value = jnp.where(part == row, low, jnp.where(part == second, high, 0.0))
                    value = jnp.where(
                        me == row, sel[i, me * each + j, :, d * half:(d + 1) * half], value
                    )
                    spread[i, row * quarter:(row + 1) * quarter, d * half:(d + 1) * half] = value
            whole = spread[i]
            whole = jnp.where(known, whole, whole.T)
            p[i, j] = whole
            chosen = STAT_DECAY * whole + (1.0 - STAT_DECAY) * gg[i, j]
            frobenius = jnp.sqrt(jnp.sum(chosen * chosen, keepdims=True))
            mat[chain + i] = chosen / frobenius
            root[chain + i] = jnp.where(diagonal, 1.0 / jnp.sqrt(jnp.sqrt(frobenius)), 0.0)

    def finish(j, chain):
        for i in (0, 1):
            flag = mk[i, pl.ds(me * each + j, 1), :] > 0.5
            for d in (0, 1):
                out[i, j, :, d * half:(d + 1) * half] = jnp.where(
                    flag,
                    root[chain + i, :, d * half:(d + 1) * half],
                    p[i, j, :, d * half:(d + 1) * half],
                )
        out[2, j] = mm(mm(out[0, j], gf[j]), out[1, j])
        begin(o_copy, j)
        o_own(j).start()

    gram(0)

    pairs = ITERS // 2
    lag = 2
    chains = range(4)

    @pl.loop(0, 2 * pairs + lag)
    def _(t):
        @pl.when(lax.rem(t, pairs) == 0)
        def _():
            @pl.when(t < 2 * pairs)
            def _():
                prepare(2 * (t // pairs), 0)

        @pl.when(lax.rem(t, pairs) == lag)
        def _():
            prepare(2 * (t // pairs) + 1, 2)

        factor = [jnp.where(diagonal, 1.25, 0.0) - 0.25 * mat[i] for i in chains]
        square = [mm(f, f) for f in factor]
        fourth = [mm(s, s) for s in square]
        term = [mm(q, 5.0 * f - 4.0 * s) for q, f, s in zip(fourth, factor, square)]
        joint = [1.25 * f - 0.25 * u for f, u in zip(factor, term)]
        product = [mm(root[i], joint[i]) for i in chains]
        for i in chains:
            root[i] = product[i]
        square = [mm(f, f) for f in joint]
        fourth = [mm(s, s) for s in square]
        matrix = [mm(fourth[i], mat[i]) for i in chains]
        for i in chains:
            mat[i] = matrix[i]

        @pl.when(lax.rem(t, pairs) == pairs - 1)
        def _():
            finish(2 * (t // pairs), 0)

        @pl.when(lax.rem(t, pairs) == lag - 1)
        def _():
            @pl.when(t >= pairs)
            def _():
                finish(2 * (t // pairs) - 1, 2)

        def at(step, *actions):
            @pl.when(t == step)
            def _():
                for action, *rest in actions:
                    action(*rest)

        at(0, (forward, g_copy, 2), (forward, s_copy, 2), (gram, 1))
        at(1, (forward, g_copy, 3), (forward, s_copy, 3))
        at(2, (forward, q_copy, 0), (gram, 2))
        at(3, (gram, 3))
        at(4, (forward, q_copy, 1))
        at(6, (forward, q_copy, 2))
        at(7, (forward, q_copy, 3))
        at(8, (forward, o_copy, 0))
        at(10, (forward, o_copy, 1))

    forward(o_copy, 2)
    forward(o_copy, 3)

    @pl.loop(0, each)
    def _(j):
        q_own(j).wait()
        arrived(q_copy, j)

    @pl.loop(0, blocks)
    def _(b):
        for side in (0, 1):
            rg[side, b] = STAT_DECAY * st[side, b] + (1.0 - STAT_DECAY) * rg[side, b]

    statistics = pltpu.make_async_copy(rg, stats_out, own_sem.at[1])
    statistics.start()

    @pl.loop(0, each)
    def _(j):
        for copy in (g_copy, s_copy, q_copy, o_copy):
            for d in (0, 1):
                for stage in (0, 1, 2):
                    copy(d, stage, j).wait_send()
        arrived(o_copy, j)
        o_own(j).wait()

    statistics.wait()


def local(n, gradients, left_stats, right_stats, left_roots, right_roots, due_factors, block_owner):
    blocks, quarter, extent = gradients.shape
    each = blocks // n
    half = extent // 2
    anywhere = pl.BlockSpec(memory_space=pl.ANY)
    dma = pltpu.SemaphoreType.DMA
    words = due_factors.shape[0], block_owner.shape[0]
    stats, results = pl.pallas_call(
        functools.partial(kernel, n),
        out_shape=(
            jax.ShapeDtypeStruct((2, blocks, quarter, extent), F32),
            jax.ShapeDtypeStruct((3, blocks, quarter, extent), F32),
        ),
        in_specs=[anywhere] * 7,
        out_specs=(anywhere, anywhere),
        scratch_shapes=[
            pltpu.VMEM((1, words[0]), jnp.int32),
            pltpu.VMEM((1, words[1]), jnp.int32),
            pltpu.VMEM((each, extent, extent), F32),
            pltpu.VMEM((2, blocks, quarter, extent), F32),
            pltpu.VMEM((2, blocks, quarter, extent), F32),
            pltpu.VMEM((2, blocks, quarter, extent), F32),
            pltpu.VMEM((blocks, 2, quarter, half), F32),
            pltpu.VMEM((n, each, 2, quarter, half), F32),
            pltpu.VMEM((2, each, extent, extent), F32),
            pltpu.VMEM((2, each, extent, extent), F32),
            pltpu.VMEM((2, blocks, quarter, extent), F32),
            pltpu.VMEM((3, each, extent, extent), F32),
            pltpu.VMEM((2, blocks, half), F32),
            pltpu.VMEM((2, each, quarter, half), F32),
            pltpu.VMEM((2, each, quarter, half), F32),
            pltpu.VMEM((2, each, 2, quarter, half), F32),
            pltpu.VMEM((2, each, 3, quarter, half), F32),
            pltpu.VMEM((2, extent, extent), F32),
            pltpu.VMEM((4, extent, extent), F32),
            pltpu.VMEM((4, extent, extent), F32),
            dma((6,)),
            dma((2,)),
            dma((2, each)),
        ] + [dma((2, 3, each))] * 8,
        compiler_params=pltpu.CompilerParams(
            collective_id=0, has_side_effects=True, vmem_limit_bytes=VMEM_LIMIT
        ),
        cost_estimate=pl.CostEstimate(
            flops=280 * 3 * 2 * extent ** 3, bytes_accessed=10 * 4 * blocks * quarter * extent, transcendentals=0
        ),
    )(
        gradients, left_stats, right_stats, left_roots, right_roots,
        due_factors.reshape(1, -1), block_owner.reshape(1, -1),
    )
    return (stats[0], stats[1], results[0], results[1], results[2])


def solution(mesh):
    spec = P("dp", "shard", None)
    return jax.shard_map(
        functools.partial(local, mesh.shape["shard"]),
        mesh=mesh,
        in_specs=(spec,) * 5 + (P(), P()),
        out_specs=(spec,) * 5,
        check_vma=False,
    )
```

time: 462 us -> 90.8 us (0.20)
  waiting for transfers between devices: 295 us -> 0 us
  Pallas kernels: 0 us -> 85 us
  matrix products: 77 us -> 0 us
  starting transfers between devices: 23.6 us -> 0 us
  blocking collectives: 17.1 us -> 0 us
  local copies, waits for them, and re-layouts: 19.2 us -> 4.94 us
  between operations: 14.3 us -> 0.64 us
  other arithmetic: 13.1 us -> 0 us
    all_to_all x3 -> x0, waiting for transfers between devices: 201 us -> none  [the longest x1 93 us: local(): lax.all_to_all(outgoing, 'dp', split_axis=0, concat_axis=0, tiled=True)]
    all_gather x2 -> x0, waiting for transfers between devices: 93.1 us -> none  [the longest x1 50.1 us: local(): gathered = lax.all_gather(gradients, 'shard', axis=1, tiled=True)]
    pallas_call x0 -> x1, Pallas kernels: none -> 85 us  [local(): pl.pallas_call(functools.partial(kernel, n), out_shape=(jax.ShapeDtypeStr...]
    dot_general x44 -> x0, matrix products: 77 us -> none  [the longest x10 18.9 us: newton_step(): jnp.einsum('...ij,...jk->...ik', iterate, factor, precision=PRECISE)]
    all_to_all x3 -> x0, starting transfers between devices: 23.3 us -> none  [the longest x1 10.5 us: local(): lax.all_to_all(outgoing, 'dp', split_axis=0, concat_axis=0, tiled=True)]
    all_to_all x1 -> x0, blocking collectives: 17.1 us -> none  [local(): lax.all_to_all(root_stack, 'shard', split_axis=2, concat_axis=0, tiled=True)]
    gather x3 -> x0, local copies, waits for them, and re-layouts: 8.46 us -> none  [the longest x1 2.87 us: local(): refreshed = jnp.take(returned, address_of, axis=0)]
    select_n x8 -> x0, other arithmetic: 8.04 us -> none  [the longest x1 4.65 us: local(): jnp.where(occupied[:, None, None], jnp.take(statistics, picked, axis=0),...]
  transfers between devices with their start and end apart: 5 -> 0, of which waited for: 5 -> 0; matrix products, arithmetic and copies ran while one was open for 2% -> 0% of each run, Pallas kernels for 0% -> 0%
where the time goes in v1:
time: 90.8 us; the launch traced here: 90.6 us
  Pallas kernels  85 us (94%)
  local copies, waits for them, and re-layouts  4.94 us (5%)
    pallas_call x1, Pallas kernels, local(): pl.pallas_call(functools.partial(kernel, n), out_shape=(jax.ShapeDtypeStr...  85 us
    squeeze x1, local copies, waits for them, and re-layouts, local(): return (stats[0], stats[1], results[0], results[1], results[2])  4.94 us

profile of v1, /device:TPU:104, one launch (start us, length us, event | category | flops | bytes accessed | tf_op | source)
XLA Modules:
  0.0 90.6 jit_solution(9569014152990629593)
XLA Ops:
  0.6 85.0 %shard_map.110 = (f32[2,16,64,256]{3,2,1,0:T(8,128)}, f32[3,16,64,256]{3,2,1,0:T(8,128)}) custom-call(f32[16,64,256]{2,1,0:T(8,128)} %g.1, f32[16,64,256]{2,1,0:T(8,128)} %ls.1, f32[16,64,256]{2,1,0:T(8,128)} %rs.1, f32[16,64,256]{2,1,0:T(8,128)} %lr.1, f32[16,64,256]{2,1,0:T(8,128)} %rr.1, s32[1,1024]{1,0:T(1,128)} %bitcast.12, s32[1,1024]{1,0:T(1,128)} %bitcast.13), custom_call_target="tpu_custom_call" | custom-call | flops 28185722880 | bytes 10485760 | tf_op jit(solution)/shard_map/pallas_call | solution.py:333
  85.6 4.9 %slice_bitcast_fusion = (f32[16,64,256]{2,1,0:T(8,128)}, f32[16,64,256]{2,1,0:T(8,128)}, f32[16,64,256]{2,1,0:T(8,128)}, f32[16,64,256]{2,1,0:T(8,128)}, f32[16,64,256]{2,1,0:T(8,128)}) fusion(f32[3,16,64,256]{3,2,1,0:T(8,128)} %get-tuple-element.8, f32[2,16,64,256]{3,2,1,0:T(8,128)} %get-tuple-element.7), kind=kLoop, calls=%fused_computation | loop fusion | bytes 10485760 | tf_op jit(solution)/shard_map/squeeze | solution.py:376

commit v2 on v1

--- a/solution.py
+++ b/solution.py
@@ -15,19 +15,51 @@
 BF16 = jnp.bfloat16
 
 
+def split(a):
+    high = a.astype(BF16)
+    low = (a - high.astype(F32)).astype(BF16)
+    return high, low
+
+
+def dot(a, b):
+    return jnp.dot(a, b, preferred_element_type=F32)
+
+
 def mm(a, b):
-    return jnp.dot(a, b, precision=lax.Precision.HIGH, preferred_element_type=F32)
+    ah, al = a
+    bh, bl = b
+    rows = ah.shape[0]
+    both = dot(jnp.concatenate([ah, al], axis=0), bh)
+    return both[:rows] + both[rows:] + dot(ah, bl)
+
+
+def mirrored(a, b):
+    ah, al = a
+    rows = ah.shape[0]
+    both = dot(jnp.concatenate([ah, al], axis=0), b[0])
+    low = both[rows:]
+    return both[:rows] + (low + low.T)
+
+
+def mirrored_and(a, x):
+    (ah, al), (xh, xl) = a, x
+    rows = ah.shape[0]
+    all_four = dot(jnp.concatenate([ah, al, xh, xl], axis=0), ah)
+    low = all_four[rows:2 * rows]
+    square = all_four[:rows] + (low + low.T)
+    product = all_four[2 * rows:3 * rows] + all_four[3 * rows:] + dot(xh, al)
+    return square, product
 
 
 def kernel(
     n,
     g, ls, rs, lr, rr, due, own,
-    stats_out, roots_out,
-    duev, ownv, gf, st, rt, sel, spk, pk, p, gg, rg, out, mk,
-    fg, fs, fgg, fo,
+    stats_out, roots_out, update_out,
+    duev, ownv, gf, st, rt, sel, spk, pk, p, gg, rg, out, ro, upd, mk,
+    fg, fs, fu, gp, gm, gx, rp, rm, rx,
     spread, mat, root,
-    load_sem, own_sem, done_sem,
-    g_send, g_recv, s_send, s_recv, q_send, q_recv, o_send, o_recv,
+    load_sem, own_sem, keep_sem,
+    g_send, g_recv, s_send, s_recv, q_send, q_recv, r_send, r_recv, u_send, u_recv,
 ):
     blocks, quarter, extent = g.shape
     each = blocks // n
@@ -67,21 +99,88 @@
             (fs.at[d, j], pk.at[origin, j, d], s_send.at[d, 2, j], s_recv.at[d, 2, j], device),
         )[stage])
 
-    def q_copy(d, stage, j):
+    def u_copy(d, stage, j):
         device, origin = sides[d]
         return remote(*(
-            (gg.at[:, j, rows(opposite), cols(d)], fgg.at[d, j], q_send.at[d, 0, j], q_recv.at[d, 0, j], device),
-            (gg.at[:, j, rows(device), :], rg.at[:, me * each + j], q_send.at[d, 1, j], q_recv.at[d, 1, j], device),
-            (fgg.at[d, j], rg.at[:, origin * each + j, :, cols(d)], q_send.at[d, 2, j], q_recv.at[d, 2, j], device),
+            (upd.at[j, rows(opposite), cols(d)], fu.at[d, j], u_send.at[d, 0, j], u_recv.at[d, 0, j], device),
+            (upd.at[j, rows(device), :], update_out.at[me * each + j], u_send.at[d, 1, j], u_recv.at[d, 1, j], device),
+            (fu.at[d, j], update_out.at[origin * each + j, :, cols(d)], u_send.at[d, 2, j], u_recv.at[d, 2, j], device),
         )[stage])
 
-    def o_copy(d, stage, j):
-        device, origin = sides[d]
-        return remote(*(
-            (out.at[:, j, rows(opposite), cols(d)], fo.at[d, j], o_send.at[d, 0, j], o_recv.at[d, 0, j], device),
-            (out.at[:, j, rows(device), :], roots_out.at[:, me * each + j], o_send.at[d, 1, j], o_recv.at[d, 1, j], device),
-            (fo.at[d, j], roots_out.at[:, origin * each + j, :, cols(d)], o_send.at[d, 2, j], o_recv.at[d, 2, j], device),
-        )[stage])
+    low_lanes = lax.broadcasted_iota(jnp.int32, (quarter, half), 1) < quarter
+
+    def place(value, parity, to):
+        return jnp.where(parity == to, value, pltpu.roll(value, quarter, 1))
+
+    def pick(first, second, index, to):
+        return place(jnp.where(index // 2 == 0, first, second), lax.rem(index, 2), to)
+
+    class Mirrored:
+        def __init__(self, src, dst, packed, passing, landed, send, recv):
+            self.src, self.dst, self.packed = src, dst, packed
+            self.passing, self.landed, self.send, self.recv = passing, landed, send, recv
+
+        def copy(self, d, stage, j):
+            device, origin = sides[d]
+            src, dst = (
+                (self.packed.at[d, j], self.passing.at[d, j, 0]),
+                (self.src.at[:, j, rows(device), :], self.dst.at[:, me * each + j]),
+                (self.passing.at[d, j], self.landed.at[d, j]),
+            )[stage]
+            return remote(src, dst, self.send.at[d, stage, j], self.recv.at[d, stage, j], device)
+
+        def begin(self, j):
+            parts = [
+                [self.src[i, j, rows(opposite), e * half:(e + 1) * half] for e in (0, 1)]
+                for i in (0, 1)
+            ]
+            for d, index in ((0, me), (1, opposite)):
+                self.packed[d, j] = jnp.where(
+                    low_lanes, pick(*parts[0], index, 0), pick(*parts[1], index, 1)
+                )
+            begin(self.copy, j)
+
+        def forward(self, j):
+            for d in (0, 1):
+                device, origin = sides[d]
+                self.copy(d, 0, j).wait_recv()
+                self.copy(d, 1, j).wait_recv()
+                parts = [
+                    pick(
+                        self.dst[i, origin * each + j, :, 0:half],
+                        self.dst[i, origin * each + j, :, half:extent],
+                        device, 0,
+                    )
+                    for i in (1, 0)
+                ]
+                self.passing[d, j, 1] = jnp.concatenate(parts, axis=0).T[0:quarter, :]
+                self.copy(d, 2, j).start()
+
+        def assemble(self, j):
+            for d in (0, 1):
+                self.copy(d, 2, j).wait_recv()
+            pieces = (
+                (self.landed[0, j, 0], opposite, 0),
+                (self.landed[0, j, 1], left, 1),
+                (self.landed[1, j, 0], me, 0),
+                (self.landed[1, j, 1], right, 1),
+            )
+            for i in (0, 1):
+                placed = [
+                    (index, place(piece, lax.rem(index, 2), (where + i) % 2))
+                    for piece, index, where in pieces
+                ]
+                for e in (0, 1):
+                    part = 2 * e + jnp.where(low_lanes, 0, 1)
+                    value = placed[0][1]
+                    for index, piece in placed[1:]:
+                        value = jnp.where(part == index, piece, value)
+                    self.dst[i, opposite * each + j, :, e * half:(e + 1) * half] = value
+
+        def sent(self, j):
+            for d in (0, 1):
+                for stage in (0, 1, 2):
+                    self.copy(d, stage, j).wait_send()
 
     def begin(copy, j):
         for stage in (0, 1):
@@ -98,15 +197,49 @@
             for stage in (1, 2):
                 copy(d, stage, j).wait_recv()
 
-    def o_own(j):
-        return pltpu.make_async_copy(
-            out.at[:, j, rows(me), :], roots_out.at[:, me * each + j], done_sem.at[0, j]
-        )
+    grams = Mirrored(gg, rg, gp, gm, gx, q_send, q_recv)
+    results = Mirrored(out, ro, rp, rm, rx, r_send, r_recv)
 
     def q_own(j):
         return pltpu.make_async_copy(
-            gg.at[:, j, rows(me), :], rg.at[:, me * each + j], done_sem.at[1, j]
+            gg.at[:, j, rows(me), :], rg.at[:, me * each + j], own_sem.at[1, j]
         )
+
+    def r_own(j):
+        return pltpu.make_async_copy(
+            out.at[:, j, rows(me), :], roots_out.at[:, me * each + j], own_sem.at[2, j]
+        )
+
+    def u_own(j):
+        return pltpu.make_async_copy(
+            upd.at[j, rows(me), :], update_out.at[me * each + j], own_sem.at[3, j]
+        )
+
+    def keep(owner, j, slot):
+        return pltpu.make_async_copy(
+            ro.at[:, owner * each + j], roots_out.at[:, owner * each + j], keep_sem.at[slot, j]
+        )
+
+    def returned(j):
+        results.assemble(j)
+        for slot, owner in enumerate((left, right, opposite)):
+            keep(owner, j, slot).start()
+
+    def statistics_copy():
+        return pltpu.make_async_copy(rg, stats_out, own_sem.at[0, 1])
+
+    def statistics():
+        @pl.loop(0, each)
+        def _(j):
+            q_own(j).wait()
+            grams.assemble(j)
+
+        @pl.loop(0, blocks)
+        def _(b):
+            for side in (0, 1):
+                rg[side, b] = STAT_DECAY * st[side, b] + (1.0 - STAT_DECAY) * rg[side, b]
+
+        statistics_copy().start()
 
     loads = [
         pltpu.make_async_copy(ref, place, load_sem.at[i])
@@ -115,7 +248,7 @@
         )
     ]
     own_rows = pltpu.make_async_copy(
-        g.at[pl.ds(me * each, each)], gf.at[:, rows(me), :], own_sem.at[0]
+        g.at[pl.ds(me * each, each)], gf.at[:, rows(me), :], own_sem.at[0, 0]
     )
     for load in loads:
         load.start()
@@ -126,7 +259,6 @@
     pl.semaphore_wait(barrier, 2)
 
     begin(g_copy, 0)
-    begin(g_copy, 1)
     own_rows.start()
 
     total = own.shape[1]
@@ -145,11 +277,9 @@
     for load in loads[2:]:
         load.wait()
 
-    low_lanes = lax.broadcasted_iota(jnp.int32, (quarter, half), 1) < quarter
-
-    @pl.loop(0, blocks)
-    def _(b):
-        second = lax.rem(jnp.where(b // each == right, me + 2, me + 1), n)
+    def choose(j, owner):
+        b = owner * each + j
+        second = lax.rem(jnp.where(owner == right, me + 2, me + 1), n)
         for side in (0, 1):
             flag = mk[side, pl.ds(b, 1), :] > 0.5
             halves = []
@@ -161,22 +291,26 @@
                 )
                 sel[side, b, :, d * half:(d + 1) * half] = value
                 halves.append(value)
-            low = jnp.where(me // 2 == 0, halves[0], halves[1])
-            low = jnp.where(lax.rem(me, 2) == 0, low, pltpu.roll(low, quarter, 1))
-            high = jnp.where(second // 2 == 0, halves[0], halves[1])
-            high = jnp.where(lax.rem(second, 2) == 1, high, pltpu.roll(high, quarter, 1))
-            spk[b, side] = jnp.where(low_lanes, low, high)
-
+            spk[b, side] = jnp.where(
+                low_lanes, pick(*halves, me, 0), pick(*halves, second, 1)
+            )
+
+    def choose_all(j):
+        @pl.loop(0, n)
+        def _(owner):
+            choose(j, owner)
+
+    choose_all(0)
     begin(s_copy, 0)
-    begin(s_copy, 1)
+    begin(g_copy, 1)
+    for j in range(1, each):
+        choose_all(j)
     forward(g_copy, 0)
     forward(s_copy, 0)
+    begin(s_copy, 1)
     begin(g_copy, 2)
     begin(s_copy, 2)
     forward(g_copy, 1)
-    forward(s_copy, 1)
-    begin(g_copy, 3)
-    begin(s_copy, 3)
     own_rows.wait()
 
     row_ids = lax.broadcasted_iota(jnp.int32, (extent, extent), 0)
@@ -190,11 +324,11 @@
 
     def gram(j):
         arrived(g_copy, j)
-        straight = gf[j]
-        turned = straight.T
-        gg[0, j] = mm(straight, turned)
-        gg[1, j] = mm(turned, straight)
-        begin(q_copy, j)
+        grad = gf[j]
+        straight, turned = split(grad), split(grad.T)
+        gg[0, j] = mirrored(straight, turned)
+        gg[1, j] = mirrored(turned, straight)
+        grams.begin(j)
         q_own(j).start()
 
     def prepare(j, chain):
@@ -233,51 +367,44 @@
                     root[chain + i, :, d * half:(d + 1) * half],
                     p[i, j, :, d * half:(d + 1) * half],
                 )
-        out[2, j] = mm(mm(out[0, j], gf[j]), out[1, j])
-        begin(o_copy, j)
-        o_own(j).start()
+        results.begin(j)
+        r_own(j).start()
+        middle = mm(split(out[0, j]), split(gf[j]))
+        upd[j] = mm(split(middle), split(out[1, j]))
+        begin(u_copy, j)
+        u_own(j).start()
 
     gram(0)
+    prepare(0, 0)
+    forward(s_copy, 1)
+    begin(g_copy, 3)
+    begin(s_copy, 3)
+
+    def body():
+        chains = range(4)
+        factor = [jnp.where(diagonal, 1.25, 0.0) - 0.25 * mat[i] for i in chains]
+        parts = [split(f) for f in factor]
+        square = [mirrored(f, f) for f in parts]
+        parts = [split(f) for f in square]
+        fourth = [mirrored(f, f) for f in parts]
+        term = [
+            mm(split(q), split(5.0 * f - 4.0 * s))
+            for q, f, s in zip(fourth, factor, square)
+        ]
+        joint = [split(1.25 * f - 0.25 * u) for f, u in zip(factor, term)]
+        both = [mirrored_and(joint[i], split(root[i])) for i in chains]
+        parts = [split(square) for square, _ in both]
+        fourth = [mirrored(f, f) for f in parts]
+        matrix = [mm(split(fourth[i]), split(mat[i])) for i in chains]
+        for i in chains:
+            root[i] = both[i][1]
+            mat[i] = matrix[i]
 
     pairs = ITERS // 2
-    lag = 2
-    chains = range(4)
-
-    @pl.loop(0, 2 * pairs + lag)
+
+    @pl.loop(0, 2 * pairs + 1)
     def _(t):
-        @pl.when(lax.rem(t, pairs) == 0)
-        def _():
-            @pl.when(t < 2 * pairs)
-            def _():
-                prepare(2 * (t // pairs), 0)
-
-        @pl.when(lax.rem(t, pairs) == lag)
-        def _():
-            prepare(2 * (t // pairs) + 1, 2)
-
-        factor = [jnp.where(diagonal, 1.25, 0.0) - 0.25 * mat[i] for i in chains]
-        square = [mm(f, f) for f in factor]
-        fourth = [mm(s, s) for s in square]
-        term = [mm(q, 5.0 * f - 4.0 * s) for q, f, s in zip(fourth, factor, square)]
-        joint = [1.25 * f - 0.25 * u for f, u in zip(factor, term)]
-        product = [mm(root[i], joint[i]) for i in chains]
-        for i in chains:
-            root[i] = product[i]
-        square = [mm(f, f) for f in joint]
-        fourth = [mm(s, s) for s in square]
-        matrix = [mm(fourth[i], mat[i]) for i in chains]
-        for i in chains:
-            mat[i] = matrix[i]
-
-        @pl.when(lax.rem(t, pairs) == pairs - 1)
-        def _():
-            finish(2 * (t // pairs), 0)
-
-        @pl.when(lax.rem(t, pairs) == lag - 1)
-        def _():
-            @pl.when(t >= pairs)
-            def _():
-                finish(2 * (t // pairs) - 1, 2)
+        body()
 
         def at(step, *actions):
             @pl.when(t == step)
@@ -285,42 +412,54 @@
                 for action, *rest in actions:
                     action(*rest)
 
-        at(0, (forward, g_copy, 2), (forward, s_copy, 2), (gram, 1))
-        at(1, (forward, g_copy, 3), (forward, s_copy, 3))
-        at(2, (forward, q_copy, 0), (gram, 2))
-        at(3, (gram, 3))
-        at(4, (forward, q_copy, 1))
-        at(6, (forward, q_copy, 2))
-        at(7, (forward, q_copy, 3))
-        at(8, (forward, o_copy, 0))
-        at(10, (forward, o_copy, 1))
-
-    forward(o_copy, 2)
-    forward(o_copy, 3)
+        @pl.when(t < pairs - 1)
+        def _():
+            at(0, (forward, g_copy, 2), (forward, s_copy, 2), (gram, 1), (prepare, 1, 2))
+            at(1, (forward, g_copy, 3), (forward, s_copy, 3), (gram, 2))
+            at(2, (grams.forward, 0), (gram, 3))
+            at(3, (grams.forward, 1))
+
+        @pl.when(t >= pairs - 1)
+        def _():
+            @pl.when(lax.rem(t, pairs) == pairs - 1)
+            def _():
+                finish(2 * (t // pairs), 0)
+
+            @pl.when(lax.rem(t, pairs) == 0)
+            def _():
+                finish(2 * (t // pairs) - 1, 2)
+
+            at(pairs - 1, (prepare, 2, 0))
+            at(pairs, (prepare, 3, 2), (grams.forward, 2))
+            at(6, (grams.forward, 3))
+            at(7, (results.forward, 0), (forward, u_copy, 0))
+            at(8, (results.forward, 1), (forward, u_copy, 1))
+
+    for j in (2, 3):
+        results.forward(j)
+        forward(u_copy, j)
+
+    statistics()
 
     @pl.loop(0, each)
     def _(j):
-        q_own(j).wait()
-        arrived(q_copy, j)
-
-    @pl.loop(0, blocks)
-    def _(b):
-        for side in (0, 1):
-            rg[side, b] = STAT_DECAY * st[side, b] + (1.0 - STAT_DECAY) * rg[side, b]
-
-    statistics = pltpu.make_async_copy(rg, stats_out, own_sem.at[1])
-    statistics.start()
+        returned(j)
 
     @pl.loop(0, each)
     def _(j):
-        for copy in (g_copy, s_copy, q_copy, o_copy):
+        for copy in (g_copy, s_copy, u_copy):
             for d in (0, 1):
                 for stage in (0, 1, 2):
                     copy(d, stage, j).wait_send()
-        arrived(o_copy, j)
-        o_own(j).wait()
-
-    statistics.wait()
+        grams.sent(j)
+        results.sent(j)
+        arrived(u_copy, j)
+        r_own(j).wait()
+        u_own(j).wait()
+        for slot, owner in enumerate((left, right, opposite)):
+            keep(owner, j, slot).wait()
+
+    statistics_copy().wait()
 
 
 def local(n, gradients, left_stats, right_stats, left_roots, right_roots, due_factors, block_owner):
@@ -330,14 +469,15 @@
     anywhere = pl.BlockSpec(memory_space=pl.ANY)
     dma = pltpu.SemaphoreType.DMA
     words = due_factors.shape[0], block_owner.shape[0]
-    stats, results = pl.pallas_call(
+    stats, roots, update = pl.pallas_call(
         functools.partial(kernel, n),
         out_shape=(
             jax.ShapeDtypeStruct((2, blocks, quarter, extent), F32),
-            jax.ShapeDtypeStruct((3, blocks, quarter, extent), F32),
+            jax.ShapeDtypeStruct((2, blocks, quarter, extent), F32),
+            jax.ShapeDtypeStruct((blocks, quarter, extent), F32),
         ),
         in_specs=[anywhere] * 7,
-        out_specs=(anywhere, anywhere),
+        out_specs=(anywhere,) * 3,
         scratch_shapes=[
             pltpu.VMEM((1, words[0]), jnp.int32),
             pltpu.VMEM((1, words[1]), jnp.int32),
@@ -350,19 +490,25 @@
             pltpu.VMEM((2, each, extent, extent), F32),
             pltpu.VMEM((2, each, extent, extent), F32),
             pltpu.VMEM((2, blocks, quarter, extent), F32),
-            pltpu.VMEM((3, each, extent, extent), F32),
+            pltpu.VMEM((2, each, extent, extent), F32),
+            pltpu.VMEM((2, blocks, quarter, extent), F32),
+            pltpu.VMEM((each, extent, extent), F32),
             pltpu.VMEM((2, blocks, half), F32),
             pltpu.VMEM((2, each, quarter, half), F32),
             pltpu.VMEM((2, each, quarter, half), F32),
+            pltpu.VMEM((2, each, quarter, half), F32),
+        ] + [
+            pltpu.VMEM((2, each, quarter, half), F32),
             pltpu.VMEM((2, each, 2, quarter, half), F32),
-            pltpu.VMEM((2, each, 3, quarter, half), F32),
+            pltpu.VMEM((2, each, 2, quarter, half), F32),
+        ] * 2 + [
             pltpu.VMEM((2, extent, extent), F32),
             pltpu.VMEM((4, extent, extent), F32),
             pltpu.VMEM((4, extent, extent), F32),
             dma((6,)),
-            dma((2,)),
-            dma((2, each)),
-        ] + [dma((2, 3, each))] * 8,
+            dma((4, each)),
+            dma((3, each)),
+        ] + [dma((2, 3, each))] * 10,
         compiler_params=pltpu.CompilerParams(
             collective_id=0, has_side_effects=True, vmem_limit_bytes=VMEM_LIMIT
         ),
@@ -373,7 +519,7 @@
         gradients, left_stats, right_stats, left_roots, right_roots,
         due_factors.reshape(1, -1), block_owner.reshape(1, -1),
     )
-    return (stats[0], stats[1], results[0], results[1], results[2])
+    return (stats[0], stats[1], roots[0], roots[1], update)
 
 
 def solution(mesh):

time: 90.8 us -> 87 us (0.958)
  Pallas kernels: 85 us -> 80.9 us
    pallas_call x1, Pallas kernels: 85 us -> 80.9 us  [local(): pl.pallas_call(functools.partial(kernel, n), out_shape=(jax.ShapeDtypeStr...]
    unnamed x0 -> x3, local copies, waits for them, and re-layouts: none -> 0.97 us
where the time goes in v2:
time: 87 us; the launch traced here: 86.9 us
  Pallas kernels  80.9 us (93%)
  local copies, waits for them, and re-layouts  5.36 us (6%)
    pallas_call x1, Pallas kernels, local(): pl.pallas_call(functools.partial(kernel, n), out_shape=(jax.ShapeDtypeStr...  80.9 us
    squeeze x1, local copies, waits for them, and re-layouts, local(): return (stats[0], stats[1], roots[0], roots[1], update)  4.39 us

profile of v2, /device:TPU:104, one launch (start us, length us, event | category | flops | bytes accessed | tf_op | source)
XLA Modules:
  0.0 86.9 jit_solution(16797106274574568488)
XLA Ops:
  0.6 80.9 %shard_map.110 = (f32[2,16,64,256]{3,2,1,0:T(8,128)}, f32[2,16,64,256]{3,2,1,0:T(8,128)}, f32[16,64,256]{2,1,0:T(8,128)}) custom-call(f32[16,64,256]{2,1,0:T(8,128)} %g.1, f32[16,64,256]{2,1,0:T(8,128)} %ls.1, f32[16,64,256]{2,1,0:T(8,128)} %rs.1, f32[16,64,256]{2,1,0:T(8,128)} %lr.1, f32[16,64,256]{2,1,0:T(8,128)} %rr.1, s32[1,1024]{1,0:T(1,128)} %bitcast.10, ...), custom_call_target="tpu_custom_call" | custom-call | flops 28185722880 | bytes 10485760 | tf_op jit(solution)/shard_map/pallas_call | solution.py:472
  81.6 0.0 copy-start
  81.6 4.4 %slice_bitcast_fusion = (f32[16,64,256]{2,1,0:T(8,128)}, f32[16,64,256]{2,1,0:T(8,128)}, f32[16,64,256]{2,1,0:T(8,128)}, f32[16,64,256]{2,1,0:T(8,128)}) fusion(f32[2,16,64,256]{3,2,1,0:T(8,128)} %get-tuple-element.9, f32[2,16,64,256]{3,2,1,0:T(8,128)} %get-tuple-element.8), kind=kLoop, calls=%fused_computation | loop fusion | bytes 8388608 | tf_op jit(solution)/shard_map/squeeze | solution.py:522
  86.0 0.0 copy-done
  86.0 1.0 %copy.13 = f32[16,64,256]{2,1,0:T(8,128)} copy(f32[16,64,256]{2,1,0:T(8,128)S(1)} %copy-done) | data formatting | bytes 2097152
Async XLA Ops:
  81.6 4.4 %copy-start = (f32[16,64,256]{2,1,0:T(8,128)S(1)}, f32[16,64,256]{2,1,0:T(8,128)}, u32[]{:S(2)}) copy-start(f32[16,64,256]{2,1,0:T(8,128)} %get-tuple-element.26) | copy-start | bytes 3145732

commit v3 on v2

--- a/solution.py
+++ b/solution.py
@@ -21,34 +21,14 @@
     return high, low
 
 
-def dot(a, b):
-    return jnp.dot(a, b, preferred_element_type=F32)
-
-
 def mm(a, b):
     ah, al = a
     bh, bl = b
-    rows = ah.shape[0]
-    both = dot(jnp.concatenate([ah, al], axis=0), bh)
-    return both[:rows] + both[rows:] + dot(ah, bl)
-
-
-def mirrored(a, b):
-    ah, al = a
-    rows = ah.shape[0]
-    both = dot(jnp.concatenate([ah, al], axis=0), b[0])
-    low = both[rows:]
-    return both[:rows] + (low + low.T)
-
-
-def mirrored_and(a, x):
-    (ah, al), (xh, xl) = a, x
-    rows = ah.shape[0]
-    all_four = dot(jnp.concatenate([ah, al, xh, xl], axis=0), ah)
-    low = all_four[rows:2 * rows]
-    square = all_four[:rows] + (low + low.T)
-    product = all_four[2 * rows:3 * rows] + all_four[3 * rows:] + dot(xh, al)
-    return square, product
+    return jnp.dot(
+        jnp.concatenate([ah, ah, al], axis=1),
+        jnp.concatenate([bh, bl, bh], axis=0),
+        preferred_element_type=F32,
+    )
 
 
 def kernel(
@@ -303,14 +283,16 @@
     choose_all(0)
     begin(s_copy, 0)
     begin(g_copy, 1)
-    for j in range(1, each):
-        choose_all(j)
+    choose_all(1)
     forward(g_copy, 0)
     forward(s_copy, 0)
     begin(s_copy, 1)
+    for j in range(2, each):
+        choose_all(j)
+    forward(g_copy, 1)
+    forward(s_copy, 1)
     begin(g_copy, 2)
     begin(s_copy, 2)
-    forward(g_copy, 1)
     own_rows.wait()
 
     row_ids = lax.broadcasted_iota(jnp.int32, (extent, extent), 0)
@@ -326,8 +308,8 @@
         arrived(g_copy, j)
         grad = gf[j]
         straight, turned = split(grad), split(grad.T)
-        gg[0, j] = mirrored(straight, turned)
-        gg[1, j] = mirrored(turned, straight)
+        gg[0, j] = mm(straight, turned)
+        gg[1, j] = mm(turned, straight)
         grams.begin(j)
         q_own(j).start()
 
@@ -376,29 +358,54 @@
 
     gram(0)
     prepare(0, 0)
-    forward(s_copy, 1)
     begin(g_copy, 3)
     begin(s_copy, 3)
 
+    def steps(i):
+        factor = jnp.where(diagonal, 1.25, 0.0) - 0.25 * mat[i]
+        parts = split(factor)
+        yield
+        square = mm(parts, parts)
+        yield
+        parts = split(square)
+        rest = split(5.0 * factor - 4.0 * square)
+        yield
+        fourth = mm(parts, parts)
+        yield
+        parts = split(fourth)
+        yield
+        term = mm(parts, rest)
+        yield
+        joint = split(1.25 * factor - 0.25 * term)
+        yield
+        square = mm(joint, joint)
+        yield
+        parts = split(square)
+        before = split(root[i])
+        yield
+        fourth = mm(parts, parts)
+        root[i] = mm(before, joint)
+        yield
+        parts = split(fourth)
+        rest = split(mat[i])
+        yield
+        matrix = mm(parts, rest)
+        yield
+        mat[i] = matrix
+        yield
+
     def body():
-        chains = range(4)
-        factor = [jnp.where(diagonal, 1.25, 0.0) - 0.25 * mat[i] for i in chains]
-        parts = [split(f) for f in factor]
-        square = [mirrored(f, f) for f in parts]
-        parts = [split(f) for f in square]
-        fourth = [mirrored(f, f) for f in parts]
-        term = [
-            mm(split(q), split(5.0 * f - 4.0 * s))
-            for q, f, s in zip(fourth, factor, square)
-        ]
-        joint = [split(1.25 * f - 0.25 * u) for f, u in zip(factor, term)]
-        both = [mirrored_and(joint[i], split(root[i])) for i in chains]
-        parts = [split(square) for square, _ in both]
-        fourth = [mirrored(f, f) for f in parts]
-        matrix = [mm(split(fourth[i]), split(mat[i])) for i in chains]
-        for i in chains:
-            root[i] = both[i][1]
-            mat[i] = matrix[i]
+        chains = [steps(i) for i in range(4)]
+        waiting = None
+        for stage in range(6):
+            for chain in chains:
+                if stage == 0:
+                    next(chain)
+                next(chain)
+                if waiting is not None:
+                    next(waiting)
+                waiting = chain
+        next(waiting)
 
     pairs = ITERS // 2
 

time: 87 us -> 87.6 us (level)
  no operation moved by 1% of the time
where the time goes in v3:
time: 87.6 us; the launch traced here: 87.5 us
  Pallas kernels  81.5 us (93%)
  local copies, waits for them, and re-layouts  5.36 us (6%)
    pallas_call x1, Pallas kernels, local(): pl.pallas_call(functools.partial(kernel, n), out_shape=(jax.ShapeDtypeStr...  81.5 us
    squeeze x1, local copies, waits for them, and re-layouts, local(): return (stats[0], stats[1], roots[0], roots[1], update)  4.39 us

profile of v3, /device:TPU:104, one launch (start us, length us, event | category | flops | bytes accessed | tf_op | source)
XLA Modules:
  0.0 87.5 jit_solution(570407679474696437)
XLA Ops:
  0.6 81.5 %shard_map.110 = (f32[2,16,64,256]{3,2,1,0:T(8,128)}, f32[2,16,64,256]{3,2,1,0:T(8,128)}, f32[16,64,256]{2,1,0:T(8,128)}) custom-call(f32[16,64,256]{2,1,0:T(8,128)} %g.1, f32[16,64,256]{2,1,0:T(8,128)} %ls.1, f32[16,64,256]{2,1,0:T(8,128)} %rs.1, f32[16,64,256]{2,1,0:T(8,128)} %lr.1, f32[16,64,256]{2,1,0:T(8,128)} %rr.1, s32[1,1024]{1,0:T(1,128)} %bitcast.10, ...), custom_call_target="tpu_custom_call" | custom-call | flops 28185722880 | bytes 10485760 | tf_op jit(solution)/shard_map/pallas_call | solution.py:479
  82.2 0.0 copy-start
  82.2 4.4 %slice_bitcast_fusion = (f32[16,64,256]{2,1,0:T(8,128)}, f32[16,64,256]{2,1,0:T(8,128)}, f32[16,64,256]{2,1,0:T(8,128)}, f32[16,64,256]{2,1,0:T(8,128)}) fusion(f32[2,16,64,256]{3,2,1,0:T(8,128)} %get-tuple-element.9, f32[2,16,64,256]{3,2,1,0:T(8,128)} %get-tuple-element.8), kind=kLoop, calls=%fused_computation | loop fusion | bytes 8388608 | tf_op jit(solution)/shard_map/squeeze | solution.py:529
  86.6 0.0 copy-done
  86.6 1.0 %copy.13 = f32[16,64,256]{2,1,0:T(8,128)} copy(f32[16,64,256]{2,1,0:T(8,128)S(1)} %copy-done) | data formatting | bytes 2097152
Async XLA Ops:
  82.2 4.4 %copy-start = (f32[16,64,256]{2,1,0:T(8,128)S(1)}, f32[16,64,256]{2,1,0:T(8,128)}, u32[]{:S(2)}) copy-start(f32[16,64,256]{2,1,0:T(8,128)} %get-tuple-element.26) | copy-start | bytes 3145732

commit v4 on v3

--- a/solution.py
+++ b/solution.py
@@ -36,7 +36,7 @@
     g, ls, rs, lr, rr, due, own,
     stats_out, roots_out, update_out,
     duev, ownv, gf, st, rt, sel, spk, pk, p, gg, rg, out, ro, upd, mk,
-    fg, fs, fu, gp, gm, gx, rp, rm, rx,
+    fg, fs, fu, gown, gp, gd, ga, gm, gx, rp, rm, rx,
     spread, mat, root,
     load_sem, own_sem, keep_sem,
     g_send, g_recv, s_send, s_recv, q_send, q_recv, r_send, r_recv, u_send, u_recv,
@@ -177,7 +177,82 @@
             for stage in (1, 2):
                 copy(d, stage, j).wait_recv()
 
-    grams = Mirrored(gg, rg, gp, gm, gx, q_send, q_recv)
+    def q_copy(d, stage, j):
+        device, origin = sides[d]
+        skip = 0 if j % 2 == d else quarter // 2
+        return remote(*(
+            (gp.at[d, j, skip:quarter], gm.at[d, j, skip:quarter], q_send.at[d, 0, j], q_recv.at[d, 0, j], device),
+            (gg.at[1, j, rows(device), :], rg.at[1, me * each + j], q_send.at[d, 1, j], q_recv.at[d, 1, j], device),
+            (gm.at[d, j, skip:half], gx.at[d, j, skip:half], q_send.at[d, 2, j], q_recv.at[d, 2, j], device),
+            (gd.at[d, j], ga.at[d, j], q_send.at[d, 3, j], q_recv.at[d, 3, j], device),
+        )[stage])
+
+    def fold(first, second, index):
+        middle = quarter // 2
+        return jnp.where(
+            low_lanes[0:middle], pick(first, second, index, 0)[0:middle], pick(first, second, index, 1)[middle:]
+        )
+
+    def unfold(value):
+        return jnp.concatenate([value, pltpu.roll(value, quarter, 1)], axis=0)
+
+    def halves_of(ref, i, block, where):
+        return [ref[i, block, where, e * half:(e + 1) * half] for e in (0, 1)]
+
+    def grams_begin(j):
+        lefts, rights = halves_of(gg, 0, j, rows(opposite)), halves_of(gg, 1, j, rows(opposite))
+        gp[j % 2, j] = jnp.where(low_lanes, pick(*lefts, me, 0), pick(*rights, me, 1))
+        gp[1 - j % 2, j, quarter // 2:quarter] = fold(*rights, opposite)
+        for d in (0, 1):
+            device, origin = sides[d]
+            lefts = halves_of(gg, 0, j, rows(device))
+            nexts = [lax.rem(device + k, n) for k in (1, 2, 3)]
+            gd[d, j, 0:quarter] = jnp.where(low_lanes, pick(*lefts, nexts[0], 0), pick(*lefts, nexts[1], 1))
+            gd[d, j, quarter:] = fold(*lefts, nexts[2])
+        for stage in (0, 3, 1):
+            for d in (0, 1):
+                q_copy(d, stage, j).start()
+
+    def grams_forward(j):
+        for d in (0, 1):
+            device, origin = sides[d]
+            for stage in (0, 3, 1):
+                q_copy(d, stage, j).wait_recv()
+            rights = pick(*halves_of(rg, 1, origin * each + j, slice(None)), device, 0)
+            lefts = ga[d, j, 0:quarter] if d == 0 else unfold(ga[d, j, quarter:])
+            gm[d, j, quarter:half] = jnp.concatenate([rights, lefts], axis=0).T[0:quarter, :]
+            q_copy(d, 2, j).start()
+
+    def put(i, row, pieces):
+        placed = [(index, place(piece, lax.rem(index, 2), lane)) for piece, index, lane in pieces]
+        for e in (0, 1):
+            part = 2 * e + jnp.where(low_lanes, 0, 1)
+            value = placed[0][1]
+            for index, piece in placed[1:]:
+                value = jnp.where(part == index, piece, value)
+            rg[i, row, :, e * half:(e + 1) * half] = value
+
+    def own_part(row):
+        high, low = split(gown[row])
+        def product(x, y):
+            return lax.dot_general(
+                x, jnp.concatenate([y, y], axis=0), (((1,), (1,)), ((), ())), preferred_element_type=F32
+            )
+        return product(high, high) + product(high, low) + product(low, high)
+
+    def grams_assemble(j):
+        for d in (0, 1):
+            q_copy(d, 2, j).wait_recv()
+        row = opposite * each + j
+        far, middle = gx[j % 2, j, 0:quarter], unfold(gx[1 - j % 2, j, quarter // 2:quarter])
+        near = [gx[d, j, quarter:half] for d in (0, 1)]
+        put(0, row, ((far, opposite, 0), (near[0], left, 1), (near[1], right, 1), (own_part(row), me, 0)))
+        put(1, row, ((far, opposite, 1), (near[0], left, 0), (near[1], right, 0), (middle, me, 0)))
+        for d in (0, 1):
+            row = sides[d][1] * each + j
+            first, third = ga[d, j, 0:quarter], unfold(ga[d, j, quarter:])
+            put(0, row, ((first, right, 0), (first, opposite, 1), (third, left, 0), (own_part(row), me, 0)))
+
     results = Mirrored(out, ro, rp, rm, rx, r_send, r_recv)
 
     def q_own(j):
@@ -209,10 +284,10 @@
         return pltpu.make_async_copy(rg, stats_out, own_sem.at[0, 1])
 
     def statistics():
-        @pl.loop(0, each)
-        def _(j):
+        loads[6].wait()
+        for j in range(each):
             q_own(j).wait()
-            grams.assemble(j)
+            grams_assemble(j)
 
         @pl.loop(0, blocks)
         def _(b):
@@ -224,7 +299,7 @@
     loads = [
         pltpu.make_async_copy(ref, place, load_sem.at[i])
         for i, (ref, place) in enumerate(
-            ((due, duev), (own, ownv), (ls, st.at[0]), (rs, st.at[1]), (lr, rt.at[0]), (rr, rt.at[1]))
+            ((due, duev), (own, ownv), (ls, st.at[0]), (rs, st.at[1]), (lr, rt.at[0]), (rr, rt.at[1]), (g, gown))
         )
     ]
     own_rows = pltpu.make_async_copy(
@@ -254,7 +329,7 @@
         flag = jnp.max(hit, axis=1, keepdims=True)
         mk[side] = jnp.broadcast_to(flag, (blocks, half))
 
-    for load in loads[2:]:
+    for load in loads[2:6]:
         load.wait()
 
     def choose(j, owner):
@@ -310,7 +385,7 @@
         straight, turned = split(grad), split(grad.T)
         gg[0, j] = mm(straight, turned)
         gg[1, j] = mm(turned, straight)
-        grams.begin(j)
+        grams_begin(j)
         q_own(j).start()
 
     def prepare(j, chain):
@@ -423,8 +498,8 @@
         def _():
             at(0, (forward, g_copy, 2), (forward, s_copy, 2), (gram, 1), (prepare, 1, 2))
             at(1, (forward, g_copy, 3), (forward, s_copy, 3), (gram, 2))
-            at(2, (grams.forward, 0), (gram, 3))
-            at(3, (grams.forward, 1))
+            at(2, (grams_forward, 0), (gram, 3))
+            at(3, (grams_forward, 1))
 
         @pl.when(t >= pairs - 1)
         def _():
@@ -437,8 +512,8 @@
                 finish(2 * (t // pairs) - 1, 2)
 
             at(pairs - 1, (prepare, 2, 0))
-            at(pairs, (prepare, 3, 2), (grams.forward, 2))
-            at(6, (grams.forward, 3))
+            at(pairs, (prepare, 3, 2), (grams_forward, 2))
+            at(6, (grams_forward, 3))
             at(7, (results.forward, 0), (forward, u_copy, 0))
             at(8, (results.forward, 1), (forward, u_copy, 1))
 
@@ -458,7 +533,6 @@
             for d in (0, 1):
                 for stage in (0, 1, 2):
                     copy(d, stage, j).wait_send()
-        grams.sent(j)
         results.sent(j)
         arrived(u_copy, j)
         r_own(j).wait()
@@ -466,6 +540,10 @@
         for slot, owner in enumerate((left, right, opposite)):
             keep(owner, j, slot).wait()
 
+    for j in range(each):
+        for d in (0, 1):
+            for stage in (0, 1, 2, 3):
+                q_copy(d, stage, j).wait_send()
     statistics_copy().wait()
 
 
@@ -504,18 +582,22 @@
             pltpu.VMEM((2, each, quarter, half), F32),
             pltpu.VMEM((2, each, quarter, half), F32),
             pltpu.VMEM((2, each, quarter, half), F32),
-        ] + [
+            pltpu.VMEM((blocks, quarter, extent), F32),
+            pltpu.VMEM((2, each, quarter, half), F32),
+            pltpu.VMEM((2, each, 3 * quarter // 2, half), F32),
+            pltpu.VMEM((2, each, 3 * quarter // 2, half), F32),
+            pltpu.VMEM((2, each, half, half), F32),
+            pltpu.VMEM((2, each, half, half), F32),
             pltpu.VMEM((2, each, quarter, half), F32),
             pltpu.VMEM((2, each, 2, quarter, half), F32),
             pltpu.VMEM((2, each, 2, quarter, half), F32),
-        ] * 2 + [
             pltpu.VMEM((2, extent, extent), F32),
             pltpu.VMEM((4, extent, extent), F32),
             pltpu.VMEM((4, extent, extent), F32),
-            dma((6,)),
+            dma((7,)),
             dma((4, each)),
             dma((3, each)),
-        ] + [dma((2, 3, each))] * 10,
+        ] + [dma((2, 3, each))] * 4 + [dma((2, 4, each))] * 2 + [dma((2, 3, each))] * 4,
         compiler_params=pltpu.CompilerParams(
             collective_id=0, has_side_effects=True, vmem_limit_bytes=VMEM_LIMIT
         ),

time: 87.6 us -> 86.8 us (level)
  no operation moved by 1% of the time
where the time goes in v4:
time: 86.8 us; the launch traced here: 86.7 us
  Pallas kernels  80.7 us (93%)
  local copies, waits for them, and re-layouts  5.36 us (6%)
    pallas_call x1, Pallas kernels, local(): pl.pallas_call(functools.partial(kernel, n), out_shape=(jax.ShapeDtypeStr...  80.7 us
    squeeze x1, local copies, waits for them, and re-layouts, local(): return (stats[0], stats[1], roots[0], roots[1], update)  4.39 us

profile of v4, /device:TPU:104, one launch (start us, length us, event | category | flops | bytes accessed | tf_op | source)
XLA Modules:
  0.0 86.7 jit_solution(3622979254249276446)
XLA Ops:
  0.6 80.7 %shard_map.110 = (f32[2,16,64,256]{3,2,1,0:T(8,128)}, f32[2,16,64,256]{3,2,1,0:T(8,128)}, f32[16,64,256]{2,1,0:T(8,128)}) custom-call(f32[16,64,256]{2,1,0:T(8,128)} %g.1, f32[16,64,256]{2,1,0:T(8,128)} %ls.1, f32[16,64,256]{2,1,0:T(8,128)} %rs.1, f32[16,64,256]{2,1,0:T(8,128)} %lr.1, f32[16,64,256]{2,1,0:T(8,128)} %rr.1, s32[1,1024]{1,0:T(1,128)} %bitcast.10, ...), custom_call_target="tpu_custom_call" | custom-call | flops 28185722880 | bytes 10485760 | tf_op jit(solution)/shard_map/pallas_call | solution.py:557
  81.4 0.0 copy-start
  81.4 4.4 %slice_bitcast_fusion = (f32[16,64,256]{2,1,0:T(8,128)}, f32[16,64,256]{2,1,0:T(8,128)}, f32[16,64,256]{2,1,0:T(8,128)}, f32[16,64,256]{2,1,0:T(8,128)}) fusion(f32[2,16,64,256]{3,2,1,0:T(8,128)} %get-tuple-element.9, f32[2,16,64,256]{3,2,1,0:T(8,128)} %get-tuple-element.8), kind=kLoop, calls=%fused_computation | loop fusion | bytes 8388608 | tf_op jit(solution)/shard_map/squeeze | solution.py:611
  85.8 0.0 copy-done
  85.8 1.0 %copy.13 = f32[16,64,256]{2,1,0:T(8,128)} copy(f32[16,64,256]{2,1,0:T(8,128)S(1)} %copy-done) | data formatting | bytes 2097152
Async XLA Ops:
  81.4 4.4 %copy-start = (f32[16,64,256]{2,1,0:T(8,128)S(1)}, f32[16,64,256]{2,1,0:T(8,128)}, u32[]{:S(2)}) copy-start(f32[16,64,256]{2,1,0:T(8,128)} %get-tuple-element.26) | copy-start | bytes 3145732
